TPU v7x, 512 devices: a whole 4x4x16 slice. The times are simulated.
512 devices in a mesh: row: 2 (over z_hi), head: 8 (over y, core), seq: 32 (over x, z_lo).
Axes of the slice: x: 4, y: 4, z: 16 (z_hi: 2, z_lo: 8; z = z_hi * 8 + z_lo), core: 2. Of those that a mesh axis runs over, the one named last changes fastest.
Arguments:
- queries: bfloat16 [64, 256, 3072], P(('row', 'seq'), 'head'), parts along dimension 0, may hold values from -45 to 45
- keys: bfloat16 [64, 256, 3072], P(('row', 'seq'), 'head'), parts along dimension 0, may hold values from -6 to 6
- values: bfloat16 [64, 256, 3072], P(('row', 'seq'), 'head'), parts along dimension 0, may hold values from -6 to 6
- clip_lengths: int32 [12], P('row'), parts along dimension 0, may hold values from 1 to 5120, 8192 in all
Outputs:
- attended: bfloat16 [64, 256, 3072], P(('row', 'seq'), 'head'), parts along dimension 0
There are 2 independent parts, one for each index of `row`. A program takes and returns all parts, laid end to end along the dimension named above; each array names one. Nothing has to cross between parts.
All inputs are finite; a program needn't handle non-finite values.
Results may differ from a plain program's by a relative error of at most 0.0065.
Values may be sent and summed in bfloat16 or wider, within the bound.
A program may use at most 128 MiB of HBM per device.

v0:
```python
import jax
import jax.numpy as jnp
from jax import lax
from jax.sharding import PartitionSpec as P

HEAD = 128


def clip_of(positions, ends, total_len):
    found = jnp.sum((positions[:, None] >= ends[None, :]).astype(jnp.int32), axis=1)
    valid = (positions >= 0) & (positions < total_len)
    return jnp.where(valid, found, -1)


def shards(queries, keys, values, clip_lengths):
    q_loc, k_loc, v_loc = (
        lax.all_to_all(queries, "head", split_axis=2, concat_axis=1, tiled=True),
        lax.all_to_all(keys, "head", split_axis=2, concat_axis=1, tiled=True),
        lax.all_to_all(values, "head", split_axis=2, concat_axis=1, tiled=True),
    )
    tok = q_loc.shape[1]
    width_here = q_loc.shape[2]
    heads_here = width_here // HEAD
    total_len = tok * lax.axis_size("seq")
    ends = jnp.cumsum(clip_lengths)
    first = lax.axis_index("seq") * tok
    q_ids = clip_of(first + jnp.arange(tok, dtype=jnp.int32), ends, total_len)
    query = q_loc[0].reshape(tok, heads_here, HEAD)
    paired = jnp.stack([k_loc[0], v_loc[0]])
    scale = HEAD ** (-0.5)
    start_state = (
        jnp.full((heads_here, tok), -1e30, jnp.float32),
        jnp.zeros((heads_here, tok), jnp.float32),
        jnp.zeros((heads_here, tok, HEAD), jnp.float32),
    )
    piece = lax.all_gather(paired, "seq", axis=1, tiled=True)
    rows = piece.shape[1]
    block = 512
    count = rows // block
    k_ids = clip_of(jnp.arange(rows, dtype=jnp.int32), ends, total_len)
    tiles = piece.reshape(2, count, block, width_here).transpose(1, 0, 2, 3)
    id_tiles = k_ids.reshape(count, block)

    def step(state, item):
        tile, tile_ids = item
        top, total, accum = state
        key_tile = tile[0].reshape(block, heads_here, HEAD)
        value_tile = tile[1].reshape(block, heads_here, HEAD)
        score = (
            jnp.einsum("qhd,khd->hqk", query, key_tile, preferred_element_type=jnp.float32) * scale
        )
        keep = (q_ids[:, None] == tile_ids[None, :])[None]
        score = jnp.where(keep, score, jnp.float32(-1e30))
        new_top = jnp.maximum(top, jnp.max(score, axis=2))
        weight = jnp.where(keep, jnp.exp(score - new_top[:, :, None]), jnp.float32(0.0))
        shrink = jnp.exp(top - new_top)
        total = total * shrink + jnp.sum(weight, axis=2)
        accum = accum * shrink[:, :, None] + jnp.einsum(
            "hqk,khd->hqd",
            weight.astype(jnp.bfloat16),
            value_tile,
            preferred_element_type=jnp.float32,
        )
        return ((new_top, total, accum), None)

    state = lax.scan(step, start_state, (tiles, id_tiles))[0]
    top, total, accum = state
    result = (
        (accum / total[:, :, None]).transpose(1, 0, 2).reshape(tok, width_here).astype(jnp.bfloat16)
    )
    return lax.all_to_all(result[None], "head", split_axis=1, concat_axis=2, tiled=True)


def solution(mesh):
    return jax.shard_map(
        shards,
        mesh=mesh,
        in_specs=(
            P(("row", "seq"), "head", None),
            P(("row", "seq"), "head", None),
            P(("row", "seq"), "head", None),
            P("row"),
        ),
        out_specs=P(("row", "seq"), "head", None),
        check_vma=False,
    )
```

profile of v0, /device:TPU:1, one launch (start us, length us, event | category | flops | bytes accessed | tf_op | source)
XLA Modules:
  0.0 435.1 jit_solution(12728594609108929147)
XLA Ops:
  6.5 3.3 copy.61
  10.4 17.0 %reduce.1 = bf16[3072,32]{1,0:T(8,128)(2,1)S(1)} reduce(bf16[3072,1,32]{2,1,0:T(2,128)(2,1)S(1)} %bitcast.71, bf16[]{:T(256)} %broadcast.60), dimensions={1}, to_apply=%bitcast.45.reduce_sub_computation | reduce | bytes 393218
  27.4 1.4 reshape.87
  28.8 10.2 %all-to-all-start = ((bf16[8,2,6144]{2,1,0:T(2,128)(2,1)}), bf16[8,2,6144]{2,1,0:T(2,128)(2,1)S(1)}, u32[]{:S(2)}, u32[]{:S(2)}) async-start(bf16[8,2,6144]{2,1,0:T(2,128)(2,1)} %reshape.87), calls=%async_computation | async-start | bytes 393216 | tf_op jit(solution)/shard_map/all_to_all | solution.py:18
  39.0 1.8 copy.64
  40.8 17.0 %reduce = bf16[3072,32]{1,0:T(8,128)(2,1)S(1)} reduce(bf16[3072,1,32]{2,1,0:T(2,128)(2,1)S(1)} %bitcast.75, bf16[]{:T(256)} %broadcast.60), dimensions={1}, to_apply=%bitcast.43.reduce_sub_computation | reduce | bytes 393218
  57.8 1.4 reshape.85
  59.2 4.8 %all-to-all-start.1 = ((bf16[8,2,6144]{2,1,0:T(2,128)(2,1)}), bf16[8,2,6144]{2,1,0:T(2,128)(2,1)S(1)}, u32[]{:S(2)}, u32[]{:S(2)}) async-start(bf16[8,2,6144]{2,1,0:T(2,128)(2,1)} %reshape.85), calls=%async_computation.1 | async-start | bytes 393216 | tf_op jit(solution)/shard_map/all_to_all | solution.py:19
  64.9 1.4 copy.62
  66.4 3.5 all-to-all-done.1
  70.8 1.4 copy.65
  73.2 1.8 copy.67
  75.0 17.0 %reduce.2 = bf16[3072,32]{1,0:T(8,128)(2,1)S(1)} reduce(bf16[3072,1,32]{2,1,0:T(2,128)(2,1)S(1)} %bitcast.76, bf16[]{:T(256)} %broadcast.60), dimensions={1}, to_apply=%bitcast.47.reduce_sub_computation | reduce | bytes 393218
  92.0 1.4 reshape.89
  93.4 4.2 all-to-all-start.2
  98.2 5.8 %all-to-all-done.2 = bf16[8,2,6144]{2,1,0:T(2,128)(2,1)S(1)} async-done(((bf16[8,2,6144]{2,1,0:T(2,128)(2,1)}), bf16[8,2,6144]{2,1,0:T(2,128)(2,1)S(1)}, u32[]{:S(2)}, u32[]{:S(2)}) %all-to-all-start.2) | async-done | bytes 196640 | tf_op jit(solution)/shard_map/all_to_all | solution.py:17
  104.9 1.4 copy.68
  106.4 254.7 %all-gather.2.cloned.1.call-done = bf16[2,8192,384]{2,1,0:T(8,128)(2,1)} async-done(((bf16[2,256,384]{2,1,0:T(8,128)(2,1)}), bf16[2,8192,384]{2,1,0:T(8,128)(2,1)}) %all-gather.2.cloned.1.call-update) | async-done | bytes 12582928 | tf_op jit(solution)/shard_map/all_gather | solution.py:36
  361.1 52.8 %while.15 = (s32[]{:T(128)}, f32[3,256]{1,0:T(4,128)S(1)}, f32[3,256]{1,0:T(4,128)S(1)}, f32[3,256,128]{2,1,0:T(8,128)S(1)}, s32[256]{0:T(256)S(1)}, /*index=5*/...) while((s32[]{:T(128)}, f32[3,256]{1,0:T(4,128)S(1)}, ...), condition=%wide.region_6.7_spmd.clone, body=%wide.region_3.6_spmd.clone.sunk | while | flops 205295360 | bytes 10214553 | solution.py:66
  364.6 1.2 constant_dynamic-slice_fusion.5
  367.9 1.2 constant_dynamic-slice_fusion.5
  374.5 1.2 constant_dynamic-slice_fusion.5
  414.6 1.8 reduce.3
  416.5 10.9 %all_to_all.69 = bf16[8,2,6144]{2,1,0:T(2,128)(2,1)S(1)} all-to-all(bf16[8,2,6144]{2,1,0:T(2,128)(2,1)S(1)} %reshape.91), channel_id=1, replica_groups=mesh['row'=2,'head'=8,'seq'=32] {'head'}, dimensions={0} | all-to-all | bytes 393216 | tf_op jit(solution)/shard_map/all_to_all | solution.py:71
  (215 shorter events, 54.4 us)
Async XLA Ops:
  10.4 28.6 %copy-start = (bf16[1,32,3072]{2,1,0:T(8,128)(2,1)S(1)}, bf16[1,32,3072]{2,1,0:T(8,128)(2,1)}, u32[]{:S(2)}) copy-start(bf16[1,32,3072]{2,1,0:T(8,128)(2,1)} %param.8) | copy-start | bytes 589828
  28.8 30.4 %all-to-all-start = ((bf16[8,2,6144]{2,1,0:T(2,128)(2,1)}), bf16[8,2,6144]{2,1,0:T(2,128)(2,1)S(1)}, u32[]{:S(2)}, u32[]{:S(2)}) async-start(bf16[8,2,6144]{2,1,0:T(2,128)(2,1)} %reshape.87), calls=%async_computation | async-start | bytes 393216 | tf_op jit(solution)/shard_map/all_to_all | solution.py:18
  59.2 10.7 %all-to-all-start.1 = ((bf16[8,2,6144]{2,1,0:T(2,128)(2,1)}), bf16[8,2,6144]{2,1,0:T(2,128)(2,1)S(1)}, u32[]{:S(2)}, u32[]{:S(2)}) async-start(bf16[8,2,6144]{2,1,0:T(2,128)(2,1)} %reshape.85), calls=%async_computation.1 | async-start | bytes 393216 | tf_op jit(solution)/shard_map/all_to_all | solution.py:19
  64.0 297.1 %all-gather.2.cloned.1.call-start = ((), (), s32[]{:S(2)}) async-start(), calls=%async_computation.4 | async-start | bytes 12976128 | tf_op jit(solution)/shard_map/all_gather | solution.py:36
  72.2 1.0 copy-start.1
  75.0 22.7 %copy-start.2 = (s32[6]{0:T(128)S(1)}, s32[6]{0:T(128)}, u32[]{:S(2)}) copy-start(s32[6]{0:T(128)} %param.9) | copy-start | bytes 76
  93.4 10.6 %all-to-all-start.2 = ((bf16[8,2,6144]{2,1,0:T(2,128)(2,1)}), bf16[8,2,6144]{2,1,0:T(2,128)(2,1)S(1)}, u32[]{:S(2)}, u32[]{:S(2)}) async-start(bf16[8,2,6144]{2,1,0:T(2,128)(2,1)} %reshape.89), calls=%async_computation.2 | async-start | bytes 393216 | tf_op jit(solution)/shard_map/all_to_all | solution.py:17
Sparse Core Ops, SparseCore 0:
  73.3 287.7 all-gather.1
where the time goes:
time: 436 us; the launch traced here: 435 us
  waiting for transfers between devices  264 us (61%)
  other arithmetic  61.8 us (14%)
  local copies, waits for them, and re-layouts  45.8 us (11%)
  starting transfers between devices  19.2 us (4%)
  matrix products  18.5 us (4%)
  between operations  13.7 us (3%)
  blocking collectives  10.9 us (2%)
    all_gather x1, waiting for transfers between devices, shards(): piece = lax.all_gather(paired, 'seq', axis=1, tiled=True)  255 us
    unnamed x7, other arithmetic  52.9 us
    slice x16, local copies, waits for them, and re-layouts, step(): value_tile = tile[1].reshape(block, heads_here, HEAD)  19.2 us
    unnamed x23, local copies, waits for them, and re-layouts  14.7 us
    all_to_all x1, blocking collectives, shards(): lax.all_to_all(result[None], 'head', split_axis=1, concat_axis=2, tiled=T...  10.9 us
    dot_general x16, matrix products, step(): jnp.einsum('hqk,khd->hqd', weight.astype(jnp.bfloat16), value_tile, prefe...  10.7 us
    all_to_all x1, starting transfers between devices, shards(): lax.all_to_all(keys, 'head', split_axis=2, concat_axis=1, tiled=True)  10.2 us
  transfers between devices with their start and end apart: 4, of which 3 were waited for; matrix products, arithmetic and copies ran while one was open for 10% of the time, Pallas kernels for 0%

commit v1 on v0

v1 whole, which is shorter than its diff:
```python
import jax
import jax.numpy as jnp
from jax import lax
from jax.experimental import pallas as pl
from jax.experimental.pallas import tpu as pltpu
from jax.sharding import PartitionSpec as P

HEAD = 128
NX, NY, NZ, NC = 4, 4, 8, 2
PER = 3
RUN = 32
CLIPS = 6
OFFSETS = (0, 4, 3, 5, 2, 6, 1, 7)
FAR = 131072.0
SCALE = HEAD**-0.5 * 1.4426950408889634
MESH = pl.DeviceIdType.MESH
KEYS_STEP = 4
QUERY_STEP = 4


def kernel(len_ref, q_ref, k_ref, v_ref, out_ref, kv, qs, far, score, result, *sems):
    send_kv, send_q, send_x, send_c, send_o, recv_kv, recv_q, recv_x, recv_c, recv_o = sems
    seq, head = lax.axis_index("seq"), lax.axis_index("head")
    x, z = seq // NZ, seq % NZ
    y, c = head // NC, head % NC
    mine = (y + NZ - z - 1) % NY
    active = mine < PER
    right, left, across = (x + 1) % NX, (x + 3) % NX, (x + 2) % NX

    def at(x_, y_, z_, c_):
        return {"seq": x_ * NZ + z_, "head": y_ * NC + c_}

    def remote(src, dst, send, recv, device):
        return pltpu.make_async_remote_copy(
            src_ref=src, dst_ref=dst, send_sem=send, recv_sem=recv, device_id=device, device_id_type=MESH
        )

    def landed(ref, sem):
        pltpu.make_async_copy(ref, ref, sem).wait()

    barrier = pltpu.get_barrier_semaphore()
    for dz in range(NZ):
        for dy in range(NY):
            if dz or dy:
                pl.semaphore_signal(
                    barrier, inc=1, device_id=at(x, (y + dy) % NY, (z + dz) % NZ, c), device_id_type=MESH
                )
    for device in (at(right, y, z, c), at(left, y, z, c), at(x, y, z, 1 - c)):
        pl.semaphore_signal(barrier, inc=1, device_id=device, device_id_type=MESH)
    pl.semaphore_wait(barrier, NZ * NY - 1 + 3)

    def columns(z_, h):
        return pl.ds(pl.multiple_of((z_ * PER + h) * HEAD, HEAD), HEAD)

    def outgoing(i, h, queries):
        z_ = (z + OFFSETS[i]) % NZ
        device = at(x, (z_ + 1 + h) % NY, z_, c)
        cols = columns(z_, h)
        if queries:
            return [(q_ref.at[0, :, cols], qs.at[i, y], send_q.at[i, h], recv_q.at[i], device)]
        return [
            (ref.at[0, :, cols], kv.at[n, i, x, c, y], send_kv.at[i, h, n], recv_kv.at[i], device)
            for n, ref in enumerate((k_ref, v_ref))
        ]

    def send(i, queries):
        for h in range(PER):
            for src, dst, out, into, device in outgoing(i, h, queries):
                if i == 0:
                    pl.when(mine == h)(lambda: pltpu.make_async_copy(src, dst, into).start())
                    pl.when(mine != h)(lambda: remote(src, dst, out, into, device).start())
                else:
                    remote(src, dst, out, into, device).start()

    def sent(i, queries):
        for h in range(PER):
            for src, dst, out, into, device in outgoing(i, h, queries):
                if i == 0:
                    pl.when(mine != h)(lambda: remote(src, dst, out, into, device).wait_send())
                else:
                    remote(src, dst, out, into, device).wait_send()

    for i in range(NZ):
        send(i, False)

    def along_x(i):
        own, from_left, from_right = kv.at[:, i, x, c], kv.at[0, i, left, c], kv.at[1, i, right, c]
        return [
            remote(own, own, send_x.at[i, 0], recv_x.at[i, 0], at(right, y, z, c)),
            remote(own, own, send_x.at[i, 1], recv_x.at[i, 1], at(left, y, z, c)),
            remote(from_left, from_left, send_x.at[i, 2], recv_x.at[i, 2], at(right, y, z, c)),
            remote(from_right, from_right, send_x.at[i, 3], recv_x.at[i, 3], at(left, y, z, c)),
        ]

    def to_core(i, n):
        ref = kv.at[:, i, (x, left, right, across)[n], c]
        return remote(ref, ref, send_c.at[i, n], recv_c.at[i], at(x, y, z, 1 - c))

    lane = lax.broadcasted_iota(jnp.int32, (1, HEAD), 1)
    first, last = jnp.zeros((1, HEAD), jnp.int32), jnp.full((1, HEAD), 1 << 20, jnp.int32)
    end = 0
    for n in range(CLIPS):
        start, end = end, end + len_ref[n]
        first = jnp.where(lane == n, start, first)
        last = jnp.where(lane == n, end, last)

    def within(position):
        return (position >= first) & (position < last)

    def far_keys(i):
        row = lax.broadcasted_iota(jnp.int32, (NX * NC * NY * RUN, HEAD), 0)
        slab = (z + NZ - OFFSETS[i]) % NZ
        position = ((row >> 8) << 11) + (((row >> 5) & 3) << 6) + (((row >> 7) & 1) << 5) + (row & 31) + slab * 256
        far[i] = jnp.where(within(position), 0.0, -FAR).astype(jnp.bfloat16)

    def clip_queries(i):
        row = lax.broadcasted_iota(jnp.int32, (NY * RUN, HEAD), 0)
        slab = (z + NZ - OFFSETS[i]) % NZ
        position = ((row >> 5) << 6) + (row & 31) + (x * 2048 + slab * 256 + c * 32)
        return jnp.where(within(position), 1.0, 0.0).astype(jnp.bfloat16)

    @pl.when(jnp.logical_not(active))
    def _():
        for i in range(NZ):
            sent(i, False)
            send(i, True)

    @pl.when(active)
    def _():
        for i in range(NZ):
            far_keys(i)
        for t in range(NZ + 3):
            if t < NZ:
                landed(kv.at[:, t, x, c], recv_kv.at[t])
                for copy in along_x(t)[:2]:
                    copy.start()
                to_core(t, 0).start()
                sent(t, False)
                send(t, True)
            if 1 <= t < NZ + 1:
                landed(kv.at[:, t - 1, left, c], recv_x.at[t - 1, 0])
                landed(kv.at[:, t - 1, right, c], recv_x.at[t - 1, 1])
                for copy in along_x(t - 1)[2:]:
                    copy.start()
                to_core(t - 1, 1).start()
                to_core(t - 1, 2).start()
            if 2 <= t < NZ + 2:
                landed(kv.at[0, t - 2, across, c], recv_x.at[t - 2, 2])
                landed(kv.at[1, t - 2, across, c], recv_x.at[t - 2, 3])
                to_core(t - 2, 3).start()
            if t >= 3:
                landed(kv.at[:, t - 3, :, 1 - c], recv_c.at[t - 3])

    def results(i):
        z_ = (z + NZ - OFFSETS[i]) % NZ
        dst = out_ref.at[0, :, columns(z, mine)]
        return [(result.at[i, n], dst, send_o.at[i, n], recv_o, at(x, n, z_, c)) for n in range(NY)]

    @pl.when(active)
    def _():
        keys = KEYS_STEP * NX * NC * NY * RUN
        rows = QUERY_STEP * NY * RUN
        for b in range(NZ // QUERY_STEP):
            rounds = range(b * QUERY_STEP, (b + 1) * QUERY_STEP)
            for i in rounds:
                landed(qs.at[i], recv_q.at[i])
            query = jnp.concatenate(
                [
                    qs[b * QUERY_STEP : (b + 1) * QUERY_STEP].reshape(rows, HEAD),
                    jnp.concatenate([clip_queries(i) for i in rounds], axis=0),
                ],
                axis=1,
            )

            def scores(j, top):
                part = pl.ds(j * KEYS_STEP, KEYS_STEP)
                key = jnp.concatenate([kv[0, part].reshape(keys, HEAD), far[part].reshape(keys, HEAD)], axis=1)
                got = lax.dot_general(query, key, (((1,), (1,)), ((), ())), preferred_element_type=jnp.float32)
                score[j] = got
                for n in range(keys // HEAD):
                    top = jnp.maximum(top, got[:, n * HEAD : (n + 1) * HEAD])
                return top

            steps = NZ // KEYS_STEP
            top = lax.fori_loop(0, steps, scores, jnp.full((rows, HEAD), -1e30, jnp.float32))
            top = jnp.max(top, axis=1, keepdims=True)

            def attend(j, total):
                part = pl.ds(j * KEYS_STEP, KEYS_STEP)
                weight = jnp.exp2((score[j] - top) * SCALE).astype(jnp.bfloat16)
                value = jnp.concatenate(
                    [kv[1, part].reshape(keys, HEAD), jnp.ones((keys, HEAD), jnp.bfloat16)], axis=1
                )
                return total + jnp.dot(weight, value, preferred_element_type=jnp.float32)

            total = lax.fori_loop(0, steps, attend, jnp.zeros((rows, 2 * HEAD), jnp.float32))
            ready = (total[:, :HEAD] / total[:, HEAD:]).astype(jnp.bfloat16)
            result[b * QUERY_STEP : (b + 1) * QUERY_STEP] = ready.reshape(QUERY_STEP, NY, RUN, HEAD)
            for i in rounds:
                for n, (src, dst, out, into, device) in enumerate(results(i)):
                    if i == 0:
                        pl.when(y == n)(lambda: pltpu.make_async_copy(src, dst, into).start())
                        pl.when(y != n)(lambda: remote(src, dst, out, into, device).start())
                    else:
                        remote(src, dst, out, into, device).start()

    landed(out_ref, recv_o)
    for i in range(NZ):
        sent(i, True)

    @pl.when(active)
    def _():
        for i in range(NZ):
            for copy in along_x(i):
                copy.wait_send()
            for n in range(4):
                to_core(i, n).wait_send()
            for n, (src, dst, out, into, device) in enumerate(results(i)):
                if i == 0:
                    pl.when(y != n)(lambda: remote(src, dst, out, into, device).wait_send())
                else:
                    remote(src, dst, out, into, device).wait_send()


def shards(queries, keys, values, clip_lengths):
    width = queries.shape[2]
    dma = pltpu.SemaphoreType.DMA
    query_rows, key_rows = QUERY_STEP * NY * RUN, KEYS_STEP * NX * NC * NY * RUN
    vmem = pl.BlockSpec(memory_space=pltpu.VMEM)
    return pl.pallas_call(
        kernel,
        out_shape=jax.ShapeDtypeStruct((1, RUN, width), jnp.bfloat16),
        in_specs=[pl.BlockSpec(memory_space=pltpu.SMEM), vmem, vmem, vmem],
        out_specs=vmem,
        scratch_shapes=[
            pltpu.VMEM((2, NZ, NX, NC, NY, RUN, HEAD), jnp.bfloat16),
            pltpu.VMEM((NZ, NY, RUN, HEAD), jnp.bfloat16),
            pltpu.VMEM((NZ, NX * NC * NY * RUN, HEAD), jnp.bfloat16),
            pltpu.VMEM((NZ // KEYS_STEP, query_rows, key_rows), jnp.float32),
            pltpu.VMEM((NZ, NY, RUN, HEAD), jnp.bfloat16),
            dma((NZ, PER, 2)),
            dma((NZ, PER)),
            dma((NZ, 4)),
            dma((NZ, 4)),
            dma((NZ, NY)),
            dma((NZ,)),
            dma((NZ,)),
            dma((NZ, 4)),
            dma((NZ,)),
            dma,
        ],
        compiler_params=pltpu.CompilerParams(
            collective_id=0, has_side_effects=True, vmem_limit_bytes=56 * 2**20
        ),
        cost_estimate=pl.CostEstimate(flops=2 * 1024 * 8192 * 512, bytes_accessed=2**20, transcendentals=2**23),
    )(clip_lengths, queries, keys, values)


def solution(mesh):
    spec = P(("row", "seq"), "head", None)
    return jax.shard_map(
        shards, mesh=mesh, in_specs=(spec, spec, spec, P("row")), out_specs=spec, check_vma=False
    )
```

time: 436 us -> 82.1 us (0.19)
  waiting for transfers between devices: 264 us -> 0 us
  Pallas kernels: 0 us -> 80.3 us
  other arithmetic: 61.8 us -> 0 us
  local copies, waits for them, and re-layouts: 45.8 us -> 1.62 us
  starting transfers between devices: 19.2 us -> 0 us
  matrix products: 18.5 us -> 0 us
  between operations: 13.7 us -> 0.01 us
  blocking collectives: 10.9 us -> 0 us
    all_gather x1 -> x0, waiting for transfers between devices: 255 us -> none  [shards(): piece = lax.all_gather(paired, 'seq', axis=1, tiled=True)]
    pallas_call x0 -> x1, Pallas kernels: none -> 80.3 us  [shards(): pl.pallas_call(kernel, out_shape=jax.ShapeDtypeStruct((1, RUN, width), jn...]
    unnamed x7 -> x0, other arithmetic: 52.9 us -> none
    slice x16 -> x0, local copies, waits for them, and re-layouts: 19.2 us -> none  [step(): value_tile = tile[1].reshape(block, heads_here, HEAD)]
    all_to_all x3 -> x0, starting transfers between devices: 19.2 us -> none  [the longest x1 10.2 us: shards(): lax.all_to_all(keys, 'head', split_axis=2, concat_axis=1, tiled=True)]
    dot_general x32 -> x0, matrix products: 18.5 us -> none  [the longest x16 10.7 us: step(): jnp.einsum('hqk,khd->hqd', weight.astype(jnp.bfloat16), value_tile, prefe...]
    unnamed x23 -> x1, local copies, waits for them, and re-layouts: 14.7 us -> 1.62 us
    all_to_all x1 -> x0, blocking collectives: 10.9 us -> none  [shards(): lax.all_to_all(result[None], 'head', split_axis=1, concat_axis=2, tiled=T...]
  transfers between devices with their start and end apart: 4 -> 0, of which waited for: 3 -> 0; matrix products, arithmetic and copies ran while one was open for 10% -> 0% of each run, Pallas kernels for 0% -> 0%
where the time goes in v1:
time: 82.1 us; the launch traced here: 82 us
  Pallas kernels  80.3 us (98%)
  local copies, waits for them, and re-layouts  1.62 us (2%)
    pallas_call x1, Pallas kernels, shards(): pl.pallas_call(kernel, out_shape=jax.ShapeDtypeStruct((1, RUN, width), jn...  80.3 us

profile of v1, /device:TPU:1, one launch (start us, length us, event | category | flops | bytes accessed | tf_op | source)
XLA Modules:
  0.0 82.0 jit_solution(2153539040379394488)
XLA Ops:
  0.0 80.3 %shard_map.46 = bf16[1,32,3072]{2,1,0:T(8,128)(2,1)} custom-call(s32[6]{0:T(128)} %len_ref.1, bf16[1,32,3072]{2,1,0:T(8,128)(2,1)} %q_ref.1, bf16[1,32,3072]{2,1,0:T(8,128)(2,1)} %k_ref.1, bf16[1,32,3072]{2,1,0:T(8,128)(2,1)} %v_ref.1), custom_call_target="tpu_custom_call" | custom-call | flops 8589934592 | bytes 1048576 | tf_op jit(solution)/shard_map/pallas_call | solution.py:230
  80.3 1.6 %copy.6 = bf16[1,32,3072]{2,1,0:T(8,128)(2,1)} copy(bf16[1,32,3072]{2,1,0:T(8,128)(2,1)} %shard_map.46) | data formatting | bytes 393216

commit v2 on v1

v2 whole, which is shorter than its diff:
```python
import jax
import jax.numpy as jnp
from jax import lax
from jax.experimental import pallas as pl
from jax.experimental.pallas import tpu as pltpu
from jax.sharding import PartitionSpec as P

HEAD = 128
NX, NY, NZ, NC = 4, 4, 8, 2
PER = 3
RUN = 32
CLIPS = 6
OFFSETS = (0, 1, 7, 2, 6, 3, 5, 4)
FAR = 131072.0
SCALE = HEAD**-0.5 * 1.4426950408889634
MESH = pl.DeviceIdType.MESH
KEYS = NX * NC * NY * RUN
KEYS_STEP = 2
QUERY_STEP = 2
UNITS = [(n, i) for n in (0, 2, 1) for i in range(NZ)]
WINDOW = 16
LAG = 4
SCORES_AT = 12


def kernel(len_ref, q_ref, k_ref, v_ref, out_ref, kv, qs, far, query, score, top, result, landing, *sems):
    send_z, send_x, send_c, send_o, recv_z, recv_x, recv_c, recv_o = sems
    seq, head = lax.axis_index("seq"), lax.axis_index("head")
    x, z = seq // NZ, seq % NZ
    y, c = head // NC, head % NC
    mine = (y + NZ - z - 1) % NY
    active = mine < PER
    right, left, across = (x + 1) % NX, (x + 3) % NX, (x + 2) % NX

    def at(x_, y_, z_, c_):
        return {"seq": x_ * NZ + z_, "head": y_ * NC + c_}

    def remote(src, dst, send, recv, device):
        return pltpu.make_async_remote_copy(
            src_ref=src, dst_ref=dst, send_sem=send, recv_sem=recv, device_id=device, device_id_type=MESH
        )

    def landed(ref, sem):
        pltpu.make_async_copy(ref, ref, sem).wait()

    barrier = pltpu.get_barrier_semaphore()
    for dz in range(NZ):
        for dy in range(NY):
            if dz or dy:
                pl.semaphore_signal(
                    barrier, inc=1, device_id=at(x, (y + dy) % NY, (z + dz) % NZ, c), device_id_type=MESH
                )
    for device in (at(right, y, z, c), at(left, y, z, c), at(x, y, z, 1 - c)):
        pl.semaphore_signal(barrier, inc=1, device_id=device, device_id_type=MESH)
    pl.semaphore_wait(barrier, NZ * NY - 1 + 3)

    def columns(z_, h):
        return pl.ds(pl.multiple_of((z_ * PER + h) * HEAD, HEAD), HEAD)

    def send(u):
        n, i = UNITS[u]
        z_ = (z + OFFSETS[i]) % NZ
        for h in range(PER):
            src = (k_ref, v_ref, q_ref)[n].at[0, :, columns(z_, h)]
            dst = qs.at[i, y] if n == 2 else kv.at[n, i, x, c, y]
            there = remote(src, dst, send_z.at[n, i], recv_z.at[n, i], at(x, (z_ + 1 + h) % NY, z_, c))
            if i == 0:
                pl.when(mine == h)(lambda: pltpu.make_async_copy(src, dst, recv_z.at[n, i]).start())
                pl.when(mine != h)(lambda: there.start())
            else:
                there.start()

    def sent(u):
        n, i = UNITS[u]
        if i == 0:
            pl.when(active)(lambda: landed(result.at[0, : PER - 1], send_z.at[n, i]))
            pl.when(jnp.logical_not(active))(lambda: landed(result.at[0, :PER], send_z.at[n, i]))
        else:
            landed(result.at[0, :PER], send_z.at[n, i])

    for u in range(WINDOW):
        send(u)

    def along_x(n, i):
        own, half = kv.at[n, i, x, c], NY // 2
        from_left, from_right = kv.at[n, i, left, c, :half], kv.at[n, i, right, c, half:]
        return [
            remote(own, own, send_x.at[n, i], recv_x.at[n, i, 0], at(right, y, z, c)),
            remote(own, own, send_x.at[n, i], recv_x.at[n, i, 0], at(left, y, z, c)),
            remote(from_left, from_left, send_x.at[n, i], recv_x.at[n, i, 1], at(right, y, z, c)),
            remote(from_right, from_right, send_x.at[n, i], recv_x.at[n, i, 1], at(left, y, z, c)),
        ]

    def to_core(n, i, x_):
        ref = kv.at[n, i, x_, c]
        remote(ref, ref, send_c.at[n, i], recv_c.at[n, i], at(x, y, z, 1 - c)).start()

    lane = lax.broadcasted_iota(jnp.int32, (1, HEAD), 1)
    first, last = jnp.zeros((1, HEAD), jnp.int32), jnp.full((1, HEAD), 1 << 20, jnp.int32)
    end = 0
    for n in range(CLIPS):
        start, end = end, end + len_ref[n]
        first = jnp.where(lane == n, start, first)
        last = jnp.where(lane == n, end, last)

    def within(position):
        return (position >= first) & (position < last)

    def far_keys(i):
        row = lax.broadcasted_iota(jnp.int32, (KEYS, HEAD), 0)
        slab = (z + NZ - OFFSETS[i]) % NZ
        position = ((row >> 8) << 11) + (((row >> 5) & 3) << 6) + (((row >> 7) & 1) << 5) + (row & 31) + slab * 256
        far[i] = jnp.where(within(position), 0.0, -FAR).astype(jnp.bfloat16)

    def clip_queries(i):
        row = lax.broadcasted_iota(jnp.int32, (NY * RUN, HEAD), 0)
        slab = (z + NZ - OFFSETS[i]) % NZ
        position = ((row >> 5) << 6) + (row & 31) + (x * 2048 + slab * 256 + c * 32)
        return jnp.where(within(position), 1.0, 0.0).astype(jnp.bfloat16)

    @pl.when(jnp.logical_not(active))
    def _():
        for u in range(len(UNITS)):
            sent(u)
            if u + WINDOW < len(UNITS):
                send(u + WINDOW)

    moved = [u for u in UNITS if u[0] < 2]

    @pl.when(active)
    def _():
        for i in range(NZ):
            far_keys(i)

        def step(t):
            def during(first_step, steps, do):
                if isinstance(t, int):
                    if first_step <= t < first_step + steps:
                        do((t - first_step) // NZ, (t - first_step) % NZ)
                else:
                    pl.when((t >= first_step) & (t < first_step + steps))(
                        lambda: do((t - first_step) // NZ, (t - first_step) % NZ)
                    )

            def begin(n, i):
                landed(kv.at[n, i, x, c], recv_z.at[n, i])
                for copy in along_x(n, i)[:2]:
                    copy.start()
                to_core(n, i, x)

            def forward(n, i):
                landed(kv.at[n, i, :2, c], recv_x.at[n, i, 0])
                for copy in along_x(n, i)[2:]:
                    copy.start()
                to_core(n, i, left)
                to_core(n, i, right)

            def finish(n, i):
                landed(kv.at[n, i, 0, c], recv_x.at[n, i, 1])
                to_core(n, i, across)

            during(0, 2 * NZ, begin)
            during(LAG, 2 * NZ, forward)
            during(2 * LAG, 2 * NZ, finish)

        for t in range(SCORES_AT):
            if t + WINDOW < len(UNITS):
                sent(t)
                send(t + WINDOW)
            step(t)

        for i in range(NZ):
            landed(qs.at[i], recv_z.at[2, i])
        rows = NZ * NY * RUN
        query[:, :HEAD] = qs[...].reshape(rows, HEAD)
        for i in range(NZ):
            query[i * NY * RUN : (i + 1) * NY * RUN, HEAD:] = clip_queries(i)
        top[...] = jnp.full((rows, HEAD), -1e30, jnp.float32)

        @pl.loop(0, NZ)
        def _(i):
            step(SCORES_AT + i)
            landed(kv.at[0, i, :, 1 - c], recv_c.at[0, i])
            key = jnp.concatenate([kv[0, i].reshape(KEYS, HEAD), far[i]], axis=1)
            got = lax.dot_general(query[...], key, (((1,), (1,)), ((), ())), preferred_element_type=jnp.float32)
            score[i] = got
            best = top[...]
            for n in range(KEYS // HEAD):
                best = jnp.maximum(best, got[:, n * HEAD : (n + 1) * HEAD])
            top[...] = best

        for t in range(SCORES_AT + NZ, 2 * NZ + 2 * LAG):
            step(t)
        for i in range(NZ):
            landed(kv.at[1, i, :, 1 - c], recv_c.at[1, i])

    def results(i):
        z_ = (z + NZ - OFFSETS[i]) % NZ
        dst = landing.at[z * PER + mine]
        return [(result.at[i, (y + n) % NY], dst, at(x, (y + n) % NY, z_, c)) for n in range(NY)]

    @pl.when(active)
    def _():
        keys, rows = KEYS_STEP * KEYS, QUERY_STEP * NY * RUN
        for b in reversed(range(NZ // QUERY_STEP)):
            rounds = range(b * QUERY_STEP, (b + 1) * QUERY_STEP)
            block = pl.ds(b * rows, rows)
            highest = jnp.max(top[block], axis=1, keepdims=True)

            def attend(j, total):
                weight = jnp.concatenate(
                    [
                        jnp.exp2((score[j * KEYS_STEP + n, block] - highest) * SCALE).astype(jnp.bfloat16)
                        for n in range(KEYS_STEP)
                    ],
                    axis=1,
                )
                value = kv[1, pl.ds(j * KEYS_STEP, KEYS_STEP)].reshape(keys, HEAD)
                value = jnp.concatenate([value, jnp.ones((keys, HEAD), jnp.bfloat16)], axis=1)
                return total + jnp.dot(weight, value, preferred_element_type=jnp.float32)

            total = lax.fori_loop(0, NZ // KEYS_STEP, attend, jnp.zeros((rows, 2 * HEAD), jnp.float32))
            ready = (total[:, :HEAD] / total[:, HEAD:]).astype(jnp.bfloat16)
            result[b * QUERY_STEP : (b + 1) * QUERY_STEP] = ready.reshape(QUERY_STEP, NY, RUN, HEAD)
            for i in reversed(rounds):
                for n, (src, dst, device) in enumerate(results(i)):
                    there = remote(src, dst, send_o.at[i], recv_o, device)
                    if i == 0 and n == 0:
                        pltpu.make_async_copy(src, dst, recv_o).start()
                    else:
                        there.start()

    landed(landing, recv_o)
    for g in range(NZ * PER):
        out_ref[0, :, g * HEAD : (g + 1) * HEAD] = landing[g]

    @pl.when(active)
    def _():
        for u in range(len(UNITS) - WINDOW, len(UNITS)):
            sent(u)
        for n, i in moved:
            landed(kv.at[n, i, :3, c], send_x.at[n, i])
            landed(kv.at[n, i, :, c], send_c.at[n, i])
        for i in range(NZ):
            landed(result.at[i, : NY - 1] if i == 0 else result.at[i], send_o.at[i])


def shards(queries, keys, values, clip_lengths):
    width = queries.shape[2]
    dma = pltpu.SemaphoreType.DMA
    rows = NZ * NY * RUN
    vmem = pl.BlockSpec(memory_space=pltpu.VMEM)
    return pl.pallas_call(
        kernel,
        out_shape=jax.ShapeDtypeStruct((1, RUN, width), jnp.bfloat16),
        in_specs=[pl.BlockSpec(memory_space=pltpu.SMEM), vmem, vmem, vmem],
        out_specs=vmem,
        scratch_shapes=[
            pltpu.VMEM((2, NZ, NX, NC, NY, RUN, HEAD), jnp.bfloat16),
            pltpu.VMEM((NZ, NY, RUN, HEAD), jnp.bfloat16),
            pltpu.VMEM((NZ, KEYS, HEAD), jnp.bfloat16),
            pltpu.VMEM((rows, 2 * HEAD), jnp.bfloat16),
            pltpu.VMEM((NZ, rows, KEYS), jnp.float32),
            pltpu.VMEM((rows, HEAD), jnp.float32),
            pltpu.VMEM((NZ, NY, RUN, HEAD), jnp.bfloat16),
            pltpu.VMEM((NZ * PER, RUN, HEAD), jnp.bfloat16),
            dma((3, NZ)),
            dma((2, NZ)),
            dma((2, NZ)),
            dma((NZ,)),
            dma((3, NZ)),
            dma((2, NZ, 2)),
            dma((2, NZ)),
            dma,
        ],
        compiler_params=pltpu.CompilerParams(
            collective_id=0, has_side_effects=True, vmem_limit_bytes=56 * 2**20
        ),
        cost_estimate=pl.CostEstimate(flops=2 * 1024 * 8192 * 512, bytes_accessed=2**20, transcendentals=2**23),
    )(clip_lengths, queries, keys, values)


def solution(mesh):
    spec = P(("row", "seq"), "head", None)
    return jax.shard_map(
        shards, mesh=mesh, in_specs=(spec, spec, spec, P("row")), out_specs=spec, check_vma=False
    )
```

time: 82.1 us -> 72 us (0.88)
  Pallas kernels: 80.3 us -> 70.2 us
    pallas_call x1, Pallas kernels: 80.3 us -> 70.2 us  [shards(): pl.pallas_call(kernel, out_shape=jax.ShapeDtypeStruct((1, RUN, width), jn...]
where the time goes in v2:
time: 72 us; the launch traced here: 71.9 us
  Pallas kernels  70.2 us (98%)
  local copies, waits for them, and re-layouts  1.62 us (2%)
    pallas_call x1, Pallas kernels, shards(): pl.pallas_call(kernel, out_shape=jax.ShapeDtypeStruct((1, RUN, width), jn...  70.2 us
    unnamed x1, local copies, waits for them, and re-layouts  1.62 us

profile of v2, /device:TPU:1, one launch (start us, length us, event | category | flops | bytes accessed | tf_op | source)
XLA Modules:
  0.0 71.9 jit_solution(3685119223600780411)
XLA Ops:
  0.0 70.2 %shard_map.46 = bf16[1,32,3072]{2,1,0:T(8,128)(2,1)} custom-call(s32[6]{0:T(128)} %len_ref.1, bf16[1,32,3072]{2,1,0:T(8,128)(2,1)} %q_ref.1, bf16[1,32,3072]{2,1,0:T(8,128)(2,1)} %k_ref.1, bf16[1,32,3072]{2,1,0:T(8,128)(2,1)} %v_ref.1), custom_call_target="tpu_custom_call" | custom-call | flops 8589934592 | bytes 1048576 | tf_op jit(solution)/shard_map/pallas_call | solution.py:253
  70.2 1.6 %copy.6 = bf16[1,32,3072]{2,1,0:T(8,128)(2,1)} copy(bf16[1,32,3072]{2,1,0:T(8,128)(2,1)} %shard_map.46) | data formatting | bytes 393216

commit v3 on v2

--- a/solution.py
+++ b/solution.py
@@ -15,12 +15,13 @@
 SCALE = HEAD**-0.5 * 1.4426950408889634
 MESH = pl.DeviceIdType.MESH
 KEYS = NX * NC * NY * RUN
-KEYS_STEP = 2
+KEYS_STEP = 4
 QUERY_STEP = 2
 UNITS = [(n, i) for n in (0, 2, 1) for i in range(NZ)]
 WINDOW = 16
-LAG = 4
-SCORES_AT = 12
+PAIRS = NZ // 2
+LAG = 2
+SCORES_AT = 6
 
 
 def kernel(len_ref, q_ref, k_ref, v_ref, out_ref, kv, qs, far, query, score, top, result, landing, *sems):
@@ -81,9 +82,12 @@
     for u in range(WINDOW):
         send(u)
 
+    def pair(i):
+        return pl.ds(2 * i, 2)
+
     def along_x(n, i):
-        own, half = kv.at[n, i, x, c], NY // 2
-        from_left, from_right = kv.at[n, i, left, c, :half], kv.at[n, i, right, c, half:]
+        own, half = kv.at[n, pair(i), x, c], NY // 2
+        from_left, from_right = kv.at[n, pair(i), left, c, :half], kv.at[n, pair(i), right, c, half:]
         return [
             remote(own, own, send_x.at[n, i], recv_x.at[n, i, 0], at(right, y, z, c)),
             remote(own, own, send_x.at[n, i], recv_x.at[n, i, 0], at(left, y, z, c)),
@@ -92,7 +96,7 @@
         ]
 
     def to_core(n, i, x_):
-        ref = kv.at[n, i, x_, c]
+        ref = kv.at[n, pair(i), x_, c]
         remote(ref, ref, send_c.at[n, i], recv_c.at[n, i], at(x, y, z, 1 - c)).start()
 
     lane = lax.broadcasted_iota(jnp.int32, (1, HEAD), 1)
@@ -125,7 +129,7 @@
             if u + WINDOW < len(UNITS):
                 send(u + WINDOW)
 
-    moved = [u for u in UNITS if u[0] < 2]
+    moved = [(n, i) for n in range(2) for i in range(PAIRS)]
 
     @pl.when(active)
     def _():
@@ -136,37 +140,39 @@
             def during(first_step, steps, do):
                 if isinstance(t, int):
                     if first_step <= t < first_step + steps:
-                        do((t - first_step) // NZ, (t - first_step) % NZ)
+                        do((t - first_step) // PAIRS, (t - first_step) % PAIRS)
                 else:
                     pl.when((t >= first_step) & (t < first_step + steps))(
-                        lambda: do((t - first_step) // NZ, (t - first_step) % NZ)
+                        lambda: do((t - first_step) // PAIRS, (t - first_step) % PAIRS)
                     )
 
             def begin(n, i):
-                landed(kv.at[n, i, x, c], recv_z.at[n, i])
+                landed(kv.at[n, 2 * i, x, c], recv_z.at[n, 2 * i])
+                landed(kv.at[n, 2 * i + 1, x, c], recv_z.at[n, 2 * i + 1])
                 for copy in along_x(n, i)[:2]:
                     copy.start()
                 to_core(n, i, x)
 
             def forward(n, i):
-                landed(kv.at[n, i, :2, c], recv_x.at[n, i, 0])
+                landed(kv.at[n, pair(i), :2, c], recv_x.at[n, i, 0])
                 for copy in along_x(n, i)[2:]:
                     copy.start()
                 to_core(n, i, left)
                 to_core(n, i, right)
 
             def finish(n, i):
-                landed(kv.at[n, i, 0, c], recv_x.at[n, i, 1])
+                landed(kv.at[n, pair(i), 0, c], recv_x.at[n, i, 1])
                 to_core(n, i, across)
 
-            during(0, 2 * NZ, begin)
-            during(LAG, 2 * NZ, forward)
-            during(2 * LAG, 2 * NZ, finish)
+            during(0, 2 * PAIRS, begin)
+            during(LAG, 2 * PAIRS, forward)
+            during(2 * LAG, 2 * PAIRS, finish)
 
         for t in range(SCORES_AT):
-            if t + WINDOW < len(UNITS):
-                sent(t)
-                send(t + WINDOW)
+            for u in (2 * t, 2 * t + 1):
+                if u + WINDOW < len(UNITS):
+                    sent(u)
+                    send(u + WINDOW)
             step(t)
 
         for i in range(NZ):
@@ -177,22 +183,25 @@
             query[i * NY * RUN : (i + 1) * NY * RUN, HEAD:] = clip_queries(i)
         top[...] = jnp.full((rows, HEAD), -1e30, jnp.float32)
 
-        @pl.loop(0, NZ)
-        def _(i):
-            step(SCORES_AT + i)
-            landed(kv.at[0, i, :, 1 - c], recv_c.at[0, i])
-            key = jnp.concatenate([kv[0, i].reshape(KEYS, HEAD), far[i]], axis=1)
-            got = lax.dot_general(query[...], key, (((1,), (1,)), ((), ())), preferred_element_type=jnp.float32)
-            score[i] = got
-            best = top[...]
-            for n in range(KEYS // HEAD):
-                best = jnp.maximum(best, got[:, n * HEAD : (n + 1) * HEAD])
-            top[...] = best
-
-        for t in range(SCORES_AT + NZ, 2 * NZ + 2 * LAG):
+        @pl.loop(0, PAIRS)
+        def _(j):
+            step(SCORES_AT + j)
+            landed(kv.at[0, pair(j), :, 1 - c], recv_c.at[0, j])
+
+            @pl.loop(2 * j, 2 * j + 2)
+            def _(i):
+                key = jnp.concatenate([kv[0, i].reshape(KEYS, HEAD), far[i]], axis=1)
+                got = lax.dot_general(query[...], key, (((1,), (1,)), ((), ())), preferred_element_type=jnp.float32)
+                score[i] = got
+                best = top[...]
+                for n in range(KEYS // HEAD):
+                    best = jnp.maximum(best, got[:, n * HEAD : (n + 1) * HEAD])
+                top[...] = best
+
+        for t in range(SCORES_AT + PAIRS, 2 * PAIRS + 2 * LAG):
             step(t)
-        for i in range(NZ):
-            landed(kv.at[1, i, :, 1 - c], recv_c.at[1, i])
+        for i in range(PAIRS):
+            landed(kv.at[1, pair(i), :, 1 - c], recv_c.at[1, i])
 
     def results(i):
         z_ = (z + NZ - OFFSETS[i]) % NZ
@@ -239,8 +248,8 @@
         for u in range(len(UNITS) - WINDOW, len(UNITS)):
             sent(u)
         for n, i in moved:
-            landed(kv.at[n, i, :3, c], send_x.at[n, i])
-            landed(kv.at[n, i, :, c], send_c.at[n, i])
+            landed(kv.at[n, pair(i), :3, c], send_x.at[n, i])
+            landed(kv.at[n, pair(i), :, c], send_c.at[n, i])
         for i in range(NZ):
             landed(result.at[i, : NY - 1] if i == 0 else result.at[i], send_o.at[i])
 
@@ -265,12 +274,12 @@
             pltpu.VMEM((NZ, NY, RUN, HEAD), jnp.bfloat16),
             pltpu.VMEM((NZ * PER, RUN, HEAD), jnp.bfloat16),
             dma((3, NZ)),
-            dma((2, NZ)),
-            dma((2, NZ)),
+            dma((2, PAIRS)),
+            dma((2, PAIRS)),
             dma((NZ,)),
             dma((3, NZ)),
-            dma((2, NZ, 2)),
-            dma((2, NZ)),
+            dma((2, PAIRS, 2)),
+            dma((2, PAIRS)),
             dma,
         ],
         compiler_params=pltpu.CompilerParams(

time: 72 us -> 71.6 us (level)
  no operation moved by 1% of the time
where the time goes in v3:
time: 71.6 us; the launch traced here: 71.4 us
  Pallas kernels  69.8 us (97%)
  local copies, waits for them, and re-layouts  1.62 us (2%)
    pallas_call x1, Pallas kernels, shards(): pl.pallas_call(kernel, out_shape=jax.ShapeDtypeStruct((1, RUN, width), jn...  69.8 us
    unnamed x1, local copies, waits for them, and re-layouts  1.62 us

profile of v3, /device:TPU:1, one launch (start us, length us, event | category | flops | bytes accessed | tf_op | source)
XLA Modules:
  0.0 71.4 jit_solution(4300387234564257078)
XLA Ops:
  0.0 69.8 %shard_map.46 = bf16[1,32,3072]{2,1,0:T(8,128)(2,1)} custom-call(s32[6]{0:T(128)} %len_ref.1, bf16[1,32,3072]{2,1,0:T(8,128)(2,1)} %q_ref.1, bf16[1,32,3072]{2,1,0:T(8,128)(2,1)} %k_ref.1, bf16[1,32,3072]{2,1,0:T(8,128)(2,1)} %v_ref.1), custom_call_target="tpu_custom_call" | custom-call | flops 8589934592 | bytes 1048576 | tf_op jit(solution)/shard_map/pallas_call | solution.py:262
  69.8 1.6 %copy.6 = bf16[1,32,3072]{2,1,0:T(8,128)(2,1)} copy(bf16[1,32,3072]{2,1,0:T(8,128)(2,1)} %shard_map.46) | data formatting | bytes 393216
